TPU v7x, 256 devices: a whole 4x4x8 slice. The times are simulated.
256 devices in a mesh: seq: 64 (over y, z_hi, x), tp: 4 (over z_lo, core).
Axes of the slice: x: 4, y: 4, z: 8 (z_hi: 4, z_lo: 2; z = z_hi * 2 + z_lo), core: 2. Of those that a mesh axis runs over, the one named last changes fastest.
Arguments:
- tokens: bfloat16 [32256, 4096], P('seq'), may hold values from -6 to 6
- norm_gain: float32 [4096], replicated, may hold values from 0.5 to 1.5
- gate_weight: bfloat16 [4096, 7168], P('seq', 'tp'), may hold values from -0.09375 to 0.09375
- up_weight: bfloat16 [4096, 7168], P('seq', 'tp'), may hold values from -0.09375 to 0.09375
Outputs:
- saved_hidden: bfloat16 [32256, 7168], P('seq', 'tp')
- token_scales: float32 [32256], P('seq')
All inputs are finite; a program needn't handle non-finite values. Where the computation divides by a largest or mean magnitude, that divisor is 1e-20 or more.
Results may differ from a plain program's by a relative error of at most 0.0061.
Values may be sent and summed in bfloat16 or wider, within the bound.
A program may use at most 128 MiB of HBM per device.

v0:
```python
import jax
import jax.numpy as jnp
from jax import lax
from jax.sharding import PartitionSpec as P


def norm_rows(block, norm_gain):
    values = block.astype(jnp.float32)
    mean_square = jnp.mean(values * values, axis=1, keepdims=True)
    return (values * lax.rsqrt(mean_square + 1e-05) * norm_gain[None, :]).astype(jnp.bfloat16)


def add_rows(normed, piece):
    return jnp.dot(normed, piece, preferred_element_type=jnp.float32)


def shards(tokens, norm_gain, gate_weight, up_weight):
    normed = norm_rows(tokens, norm_gain)

    def add_single(piece):
        return add_rows(normed, piece)

    gate = add_single(lax.all_gather(gate_weight, "seq", axis=0, tiled=True))
    up = add_single(lax.all_gather(up_weight, "seq", axis=0, tiled=True))
    hidden = jax.nn.silu(gate) * up
    local_peak = jnp.max(jnp.abs(hidden), axis=1)
    scales = lax.pmax(local_peak, "tp") + 1e-06
    saved = (hidden / scales[:, None]).astype(jnp.bfloat16)
    return (saved, scales)


def solution(mesh):
    in_specs = (P("seq", None), P(), P("seq", "tp"), P("seq", "tp"))
    out_specs = (P("seq", "tp"), P("seq"))
    return jax.shard_map(shards, mesh=mesh, in_specs=in_specs, out_specs=out_specs, check_vma=False)
```

profile of v0, /device:TPU:1, one launch (start us, length us, event | category | flops | bytes accessed | tf_op | source)
XLA Modules:
  0.0 359.4 jit_solution(13655028735498425475)
XLA Ops:
  7.2 0.0 copy-start.1
  7.2 0.0 all-gather.3.cloned.1.call-start
  7.2 0.7 all-gather.3.cloned.1.call-update
  7.9 0.0 all-gather.5.cloned.1.call-start
  8.0 0.7 all-gather.5.cloned.1.call-update
  8.7 3.1 fusion
  11.7 150.1 %all-gather.3.cloned.1.call-done = bf16[4096,1792]{1,0:T(8,128)(2,1)} async-done(((bf16[64,1792]{1,0:T(8,128)(2,1)}), bf16[4096,1792]{1,0:T(8,128)(2,1)}) %all-gather.3.cloned.1.call-update) | async-done | bytes 14680080 | tf_op jit(solution)/shard_map/all_gather | solution.py:23
  161.8 0.0 copy-done.1
  161.8 14.5 %fusion.4 = f32[504,1792]{1,0:T(8,128)} fusion(bf16[4096,1792]{1,0:T(8,128)(2,1)} %all-gather.3.cloned.1.call-done, bf16[504,4096]{1,0:T(8,128)(2,1)} %param.4, f32[4096]{0:T(1024)S(1)} %copy-done.1, f32[504]{0:T(512)S(1)} %add_rsqrt_fusion), kind=kOutput, calls=%fused_computation.8 | convolution fusion | flops 7407009792 | bytes 22439904 | tf_op jit(solution)/shard_map/dot_general | solution.py:14
  176.4 142.6 %all-gather.5.cloned.1.call-done = bf16[4096,1792]{1,0:T(8,128)(2,1)} async-done(((bf16[64,1792]{1,0:T(8,128)(2,1)}), bf16[4096,1792]{1,0:T(8,128)(2,1)}) %all-gather.5.cloned.1.call-update) | async-done | bytes 14680080 | tf_op jit(solution)/shard_map/all_gather | solution.py:24
  319.0 16.1 %abs_reduce_fusion = (f32[504]{0:T(512)S(1)}, f32[504,1792]{1,0:T(8,128)}) fusion(bf16[4096,1792]{1,0:T(8,128)(2,1)} %all-gather.5.cloned.1.call-done, bf16[504,4096]{1,0:T(8,128)(2,1)} %param.4, f32[4096]{0:T(1024)S(1)} %copy-done.1, f32[504]{0:T(512)S(1)} %add_rsqrt_fusion, f32[504,1792]{1,0:T(8,128)} %fusion.4), kind=kOutput, calls=%fused_computation.6 | convolution fusion | flops 7413331456 | bytes 26054592 | tf_op jit(solution)/shard_map/dot_general | solution.py:14
  335.1 13.8 %pmax.7 = f32[504]{0:T(512)S(1)} all-reduce(f32[504]{0:T(512)S(1)} %get-tuple-element.2), channel_id=1, replica_groups=mesh['seq'=64,'tp'=4] {'tp'}, use_global_device_ids=true, to_apply=%region_2.3 | all-reduce | flops 504 | bytes 4032 | tf_op jit(solution)/shard_map/pmax | solution.py:27
  348.9 0.0 copy-start
  348.9 3.6 %divide_convert_fusion = bf16[504,1792]{1,0:T(8,128)(2,1)} fusion(f32[504,1792]{1,0:T(8,128)} %get-tuple-element.3, f32[504]{0:T(512)S(1)} %broadcast_add_fusion), kind=kLoop, calls=%fused_computation.5 | loop fusion | flops 1806336 | bytes 5421024 | tf_op jit(solution)/shard_map/convert_element_type | solution.py:28
  352.6 0.0 copy-done
  (2 shorter events, 0.0 us)
Async XLA Ops:
  7.2 154.7 %copy-start.1 = (f32[4096]{0:T(1024)S(1)}, f32[4096]{0:T(1024)}, u32[]{:S(2)}) copy-start(f32[4096]{0:T(1024)} %param.5) | copy-start | bytes 49156
  7.2 154.7 %all-gather.3.cloned.1.call-start = ((), (), s32[]{:S(2)}) async-start(), calls=%async_computation | async-start | bytes 14909440 | tf_op jit(solution)/shard_map/all_gather | solution.py:23
  7.9 311.1 %all-gather.5.cloned.1.call-start = ((), (), s32[]{:S(2)}) async-start(), calls=%async_computation.1 | async-start | bytes 14909440 | tf_op jit(solution)/shard_map/all_gather | solution.py:24
  348.9 3.6 %copy-start = (f32[504]{0:T(512)}, f32[504]{0:T(512)S(1)}, u32[]{:S(2)}) copy-start(f32[504]{0:T(512)S(1)} %broadcast_add_fusion) | copy-start | bytes 6052
Sparse Core Ops, SparseCore 0:
  11.3 150.4 all-gather.2
  165.1 153.8 all-gather.4
where the time goes:
time: 361 us; the launch traced here: 359 us
  waiting for transfers between devices  294 us (81%)
  matrix products  30.6 us (8%)
  between operations  14 us (4%)
  blocking collectives  13.8 us (4%)
  other arithmetic  6.69 us (2%)
    all_gather x1, waiting for transfers between devices, shards(): gate = add_single(lax.all_gather(gate_weight, 'seq', axis=0, tiled=True))  150 us
    all_gather x1, waiting for transfers between devices, shards(): up = add_single(lax.all_gather(up_weight, 'seq', axis=0, tiled=True))  143 us
    dot_general x2, matrix products, add_rows(): return jnp.dot(normed, piece, preferred_element_type=jnp.float32)  30.6 us
    pmax x1, blocking collectives, shards(): scales = lax.pmax(local_peak, 'tp') + 1e-06  13.8 us
  transfers between devices with their start and end apart: 2, of which 2 were waited for; matrix products, arithmetic and copies ran while one was open for 5% of the time, Pallas kernels for 0%

commit v1 on v0

v1 whole, which is shorter than its diff:
```python
import functools

import jax
import jax.numpy as jnp
from jax import lax
from jax.experimental import pallas as pl
from jax.experimental.pallas import tpu as pltpu
from jax.sharding import PartitionSpec as P

MESH = pl.DeviceIdType.MESH
TOK = 504
PAD = 512
D = 4096
PIECE = 896
NCOL = 2 * PIECE
ROWS = 128
EPS = 1e-05


def mod(v, n):
    return lax.rem(v + 2 * n, n)


def kernel(tok_hbm, gain_ref, gate_hbm, up_hbm, out_ref, scale_ref,
           raw, tok, w, acc, osend, orecv, psend, precv,
           raw_sem, s1_ss, s1_rs, t_ss, t_rs, r_ss, r_rs, z_ss, z_rs, y_ss, y_rs,
           b_ss, b_rs, o_ss, o_rs, p_ss, p_rs):
    s = lax.axis_index("seq")
    t = lax.axis_index("tp")
    x = s % 4
    zh = (s // 4) % 4
    y = s // 16
    zl = t // 2
    c = t % 2

    def dev(xx, yy, zz, ll, cc):
        return ((yy * 4 + zz) * 4 + xx, ll * 2 + cc)

    def rc(src, dst, ssem, rsem, target):
        return pltpu.make_async_remote_copy(
            src_ref=src, dst_ref=dst, send_sem=ssem, recv_sem=rsem,
            device_id=target, device_id_type=MESH)

    xp, xm = mod(x + 1, 4), mod(x - 1, 4)
    yp, ym = mod(y + 1, 4), mod(y - 1, 4)
    zp, zm = mod(zh + 1, 4), mod(zh - 1, 4)
    sib = dev(x, y, zh, zl, 1 - c)
    y_up, y_dn = dev(x, yp, zh, zl, c), dev(x, ym, zh, zl, c)
    z_up, z_dn = dev(x, y, zp, zl, c), dev(x, y, zm, zl, c)

    raw_copy = pltpu.make_async_copy(tok_hbm, raw, raw_sem)
    raw_copy.start()

    barrier = pltpu.get_barrier_semaphore()
    for dx in range(4):
        for ll in range(2):
            for cc in range(2):
                if dx == 0 and ll == 0 and cc == 0:
                    continue
                pl.semaphore_signal(
                    barrier, inc=1, device_id_type=MESH,
                    device_id=dev(mod(x + dx, 4), y, zh, (zl + ll) % 2, (c + cc) % 2))
    for target in (y_up, y_dn, z_up, z_dn):
        pl.semaphore_signal(barrier, inc=1, device_id=target, device_id_type=MESH)
    pl.semaphore_wait(barrier, 19)

    def base(zz, yy):
        return pl.multiple_of((zz * 4 + yy) * 256, 256)

    def w_part(r, n):
        return w.at[pl.ds(pl.multiple_of(r, 64), n)]

    def s1_dst(xx, g):
        return w.at[pl.ds(pl.multiple_of(base(zh, y) + xx * 64, 64), 64), pl.ds(g * PIECE, PIECE)]

    def s1_copy(h, g):
        src = (gate_hbm, up_hbm)[g].at[:, pl.ds(h * PIECE, PIECE)]
        sem = s1_rs.at[(x % 2) * 2 + g]
        return src, s1_dst(x, g), sem

    for h in range(2):
        mine = jnp.logical_and(x // 2 == c, x % 2 == h)
        for g in range(2):
            src, dst, sem = s1_copy(h, g)

            @pl.when(mine)
            def _():
                pltpu.make_async_copy(src, dst, sem).start()

            @pl.when(jnp.logical_not(mine))
            def _():
                rc(src, dst, s1_ss.at[h * 2 + g], sem, dev(2 * c + h, y, zh, zl, x // 2)).start()

    raw_copy.wait()
    gain = gain_ref[...].reshape(1, D)

    def normed(values):
        v = values.astype(jnp.float32)
        mean_square = jnp.sum(v * v, axis=1, keepdims=True) * (1.0 / D)
        return (v * lax.rsqrt(mean_square + EPS) * gain).astype(jnp.bfloat16)

    def put(r, n, val):
        for yy in range(4):
            for zz in range(4):
                a, b = (yy * 4 + zz) * 256, (zz * 4 + yy) * 256
                tok[2, pl.ds(r, n), pl.ds(b, 256)] = val[:, a:a + 256]

    def norm_group(i, carry):
        r = pl.multiple_of(i * 16, 16)
        put(r, 16, normed(raw[pl.ds(r, 16), :]))
        return carry

    def tok_chunk(slot, j):
        return tok.at[slot, pl.ds(j * ROWS, ROWS)]

    t_target = dev(mod(x + 1 - 2 * c, 4), y, zh, zl, 1)

    def t_send(j):
        return rc(tok_chunk(2, j), tok_chunk(c, j), t_ss.at[j], t_rs.at[c * 4 + j], t_target)

    for j in range(4):
        lax.fori_loop(j * 8, j * 8 + (7 if j == 3 else 8), norm_group, 0)
        if j == 3:
            tail = normed(raw[pl.ds(496, 8), :])
            put(496, 16, jnp.concatenate([tail, jnp.zeros((8, D), jnp.bfloat16)], axis=0))
        t_send(j).start()

    def chunk(zz, yy, cc):
        return w_part(base(zz, yy) + cc * 128, 128)

    def half(zz, yy, hh):
        return w_part(base(zz, yy) + c * 128 + hh * 64, 64)

    rels = (0, 1, 3, 2)
    zz_of = {r: mod(zh + r, 4) for r in rels}
    yy_of = {0: y, 1: yp, 3: ym, 2: mod(y + 2, 4)}

    def b_copy(r, q):
        ref = chunk(zz_of[r], yy_of[q], c)
        return rc(ref, ref, b_ss.at[r * 4 + q], b_rs.at[r * 4 + q], sib)

    def b_wait(r):
        for q in range(4):
            ref = chunk(zz_of[r], yy_of[q], 1 - c)
            rc(ref, ref, b_ss.at[r * 4 + q], b_rs.at[r * 4 + q], sib).wait_recv()

    def y_send(r, d):
        ref = chunk(zz_of[r], y, c)
        return rc(ref, ref, y_ss.at[r * 4 + d], y_rs.at[r * 4 + d], (y_up, y_dn)[d])

    def y_relay(r, d):
        ref = half(zz_of[r], (ym, yp)[d], d)
        return rc(ref, ref, y_ss.at[r * 4 + 2 + d], y_rs.at[r * 4 + 2 + d], (y_up, y_dn)[d])

    def y_arrived(r, d):
        ref = chunk(zz_of[r], (ym, yp)[d], c)
        rc(ref, ref, y_ss.at[r * 4 + d], y_rs.at[r * 4 + d], sib).wait_recv()

    def y_opposite(r):
        for d in range(2):
            ref = half(zz_of[r], yy_of[2], d)
            rc(ref, ref, y_ss.at[r * 4 + 2 + d], y_rs.at[r * 4 + 2 + d], sib).wait_recv()

    def z_send(d):
        ref = chunk(zh, y, c)
        return rc(ref, ref, z_ss.at[d], z_rs.at[d], (z_up, z_dn)[d])

    def z_relay(d):
        ref = half((zm, zp)[d], y, d)
        return rc(ref, ref, z_ss.at[2 + d], z_rs.at[2 + d], (z_up, z_dn)[d])

    def z_arrived(d):
        ref = chunk((zm, zp)[d], y, c)
        rc(ref, ref, z_ss.at[d], z_rs.at[d], sib).wait_recv()

    def z_opposite():
        for d in range(2):
            ref = half(zz_of[2], y, d)
            rc(ref, ref, z_ss.at[2 + d], z_rs.at[2 + d], sib).wait_recv()

    def y_step(r):
        for d in range(2):
            y_arrived(r, d)
            y_relay(r, d).start()
        b_copy(r, 3).start()
        b_copy(r, 1).start()

    def y_finish(r):
        y_opposite(r)
        b_copy(r, 2).start()
        b_wait(r)

    def t_arrived(j):
        for slot in range(2):
            ref = tok_chunk(slot, j)
            rc(ref, ref, t_ss.at[j], t_rs.at[slot * 4 + j], sib).wait_recv()

    def relay(j):
        slot = j % 2
        target = dev((xp, xm)[slot], y, zh, zl, 0)
        return rc(tok_chunk(slot, j), tok_chunk(1, j), r_ss.at[j], r_rs.at[j], target)

    def t_step(j):
        @pl.when(c == 1)
        def _():
            t_arrived(j)
            relay(j).start()

    def opp_arrived(j):
        ref = tok_chunk(1, j)
        rc(ref, ref, r_ss.at[j], r_rs.at[j], sib).wait_recv()

    first = jnp.where(c == 0, 2, 0)

    def unit(slot, r, r0=0, nr=PAD, start=False):
        src = first if slot == 0 else 1
        k0 = pl.multiple_of(zz_of[r] * 1024, 1024)

        def col(n, carry):
            cols = pl.ds(pl.multiple_of(n * 256, 256), 256)
            part = jnp.dot(tok[src, pl.ds(r0, nr), pl.ds(k0, 1024)], w[pl.ds(k0, 1024), cols],
                           preferred_element_type=jnp.float32)
            if start:
                acc[slot, pl.ds(r0, nr), cols] = part
            else:
                acc[slot, pl.ds(r0, nr), cols] += part
            return carry

        lax.fori_loop(0, NCOL // 256, col, 0)

    for p in range(2):
        for g in range(2):
            ref = s1_dst(2 * c + p, g)
            rc(ref, ref, s1_ss.at[0], s1_rs.at[p * 2 + g], sib).wait_recv()
    for d in range(2):
        y_send(0, d).start()
        z_send(d).start()
    b_copy(0, 0).start()

    t_step(0)
    y_step(0)
    t_step(1)
    for d, r in ((0, 3), (1, 1)):
        z_arrived(d)
        z_relay(d).start()
        b_copy(r, 0).start()
    for r in (1, 3):
        y_send(r, 0).start()
        y_send(r, 1).start()
    y_finish(0)

    @pl.when(c == 0)
    def _():
        unit(0, 0, start=True)

    z_opposite()
    y_send(2, 0).start()
    y_send(2, 1).start()
    b_copy(2, 0).start()
    t_step(2)
    y_step(1)
    t_step(3)

    @pl.when(c == 1)
    def _():
        unit(0, 0, start=True)
        unit(1, 0, start=True)

    y_finish(1)
    unit(0, 1)

    @pl.when(c == 1)
    def _():
        unit(1, 1)

    y_step(3)
    y_finish(3)
    unit(0, 3)

    @pl.when(c == 1)
    def _():
        unit(1, 3)

    y_step(2)

    @pl.when(c == 0)
    def _():
        for j0 in (0, 2):
            opp_arrived(j0)
            opp_arrived(j0 + 1)
            unit(1, 0, j0 * ROWS, 256, start=True)
            unit(1, 1, j0 * ROWS, 256)
            unit(1, 3, j0 * ROWS, 256)

    y_finish(2)

    def hidden(slot):
        def rows(i, carry):
            r = pl.ds(pl.multiple_of(i * ROWS, ROWS), ROWS)
            peak = jnp.zeros((ROWS, 128), jnp.float32)
            for n in range(PIECE // 128):
                gate = acc[slot, r, pl.ds(n * 128, 128)]
                up = acc[slot, r, pl.ds(PIECE + n * 128, 128)]
                val = gate / (1.0 + jnp.exp(-gate)) * up
                peak = jnp.maximum(peak, jnp.abs(val))
                osend[slot, r, pl.ds(n * 128, 128)] = val.astype(jnp.bfloat16)
            top = jnp.max(peak.T, axis=0, keepdims=True)
            psend[slot, :, r] = jnp.broadcast_to(top, (8, ROWS))
            return carry

        lax.fori_loop(0, PAD // ROWS, rows, 0)

    rel_of = (jnp.where(c == 0, 0, 3), jnp.where(c == 0, 2, 1))

    def to_owner(slot, wait):
        rel = rel_of[slot]
        xb = mod(x + rel, 4)

        def move(src, dst, ssem, rsem, ll, cc):
            here = jnp.logical_and(rel == 0, jnp.logical_and(ll == zl, cc == c))

            @pl.when(jnp.logical_not(here))
            def _():
                copy = rc(src, dst, ssem, rsem, dev(xb, y, zh, ll, cc))
                if wait:
                    copy.wait_send()
                else:
                    copy.start()

            if not wait:
                @pl.when(here)
                def _():
                    pltpu.make_async_copy(src, dst, rsem).start()

        index = rel * 2 + zl
        for k in range(4):
            move(psend.at[slot], precv.at[index], p_ss.at[slot * 4 + k], p_rs.at[index], k // 2, k % 2)
        move(osend.at[slot], orecv.at[:, pl.ds(pl.multiple_of((x % 2) * PIECE, 128), PIECE)],
             o_ss.at[slot], o_rs.at[x % 2], zl, x // 2)

    unit(0, 2)
    hidden(0)
    to_owner(0, False)

    @pl.when(c == 1)
    def _():
        unit(1, 2)

    @pl.when(c == 0)
    def _():
        unit(1, 2)

    hidden(1)
    to_owner(1, False)

    top = None
    for i in range(8):
        ref = precv.at[i]
        rc(ref, ref, p_ss.at[0], p_rs.at[i], sib).wait_recv()
    top = precv[0]
    for i in range(1, 8):
        top = jnp.maximum(top, precv[i])
    top = top + 1e-06
    scale_ref[...] = top[0, :TOK]
    psend_inv = 1.0 / top
    for p in range(2):
        ref = orecv.at[:, pl.ds(p * PIECE, PIECE)]
        rc(ref, ref, o_ss.at[0], o_rs.at[p], sib).wait_recv()
    for i in range(PAD // ROWS):
        n = min(ROWS, TOK - i * ROWS)
        inv = jnp.broadcast_to(psend_inv[:1, i * ROWS:(i + 1) * ROWS], (ROWS, ROWS)).T
        for k in range(NCOL // 128):
            val = orecv[pl.ds(i * ROWS, ROWS), pl.ds(k * 128, 128)].astype(jnp.float32) * inv
            out_ref[pl.ds(i * ROWS, n), pl.ds(k * 128, 128)] = val.astype(jnp.bfloat16)[:n]

    for h in range(2):
        mine = jnp.logical_and(x // 2 == c, x % 2 == h)
        for g in range(2):
            src, dst, sem = s1_copy(h, g)

            @pl.when(jnp.logical_not(mine))
            def _():
                rc(src, dst, s1_ss.at[h * 2 + g], sem, sib).wait_send()
    for j in range(4):
        t_send(j).wait_send()

        @pl.when(c == 1)
        def _():
            relay(j).wait_send()
    for d in range(2):
        z_send(d).wait_send()
        z_relay(d).wait_send()
        for r in rels:
            y_send(r, d).wait_send()
            y_relay(r, d).wait_send()
    for r in rels:
        for q in range(4):
            b_copy(r, q).wait_send()
    to_owner(0, True)
    to_owner(1, True)


def shards(tokens, norm_gain, gate_weight, up_weight):
    dma = pltpu.SemaphoreType.DMA
    vmem = pl.BlockSpec(memory_space=pltpu.VMEM)
    hbm = pl.BlockSpec(memory_space=pl.ANY)
    return pl.pallas_call(
        kernel,
        name="block",
        out_shape=(jax.ShapeDtypeStruct((TOK, NCOL), jnp.bfloat16),
                   jax.ShapeDtypeStruct((TOK,), jnp.float32)),
        in_specs=[hbm, vmem, hbm, hbm],
        out_specs=(vmem, vmem),
        scratch_shapes=[
            pltpu.VMEM((TOK, D), jnp.bfloat16),
            pltpu.VMEM((3, PAD, D), jnp.bfloat16),
            pltpu.VMEM((D, NCOL), jnp.bfloat16),
            pltpu.VMEM((2, PAD, NCOL), jnp.float32),
            pltpu.VMEM((2, PAD, PIECE), jnp.bfloat16),
            pltpu.VMEM((PAD, NCOL), jnp.bfloat16),
            pltpu.VMEM((2, 8, PAD), jnp.float32),
            pltpu.VMEM((8, 8, PAD), jnp.float32),
            dma, dma((4,)), dma((4,)), dma((4,)), dma((8,)), dma((4,)), dma((4,)),
            dma((4,)), dma((4,)), dma((16,)), dma((16,)), dma((16,)), dma((16,)),
            dma((2,)), dma((2,)), dma((8,)), dma((8,)),
        ],
        compiler_params=pltpu.CompilerParams(
            collective_id=0, has_side_effects=True, vmem_limit_bytes=58 * 2**20),
    )(tokens, norm_gain, gate_weight, up_weight)


def solution(mesh):
    in_specs = (P("seq", None), P(), P("seq", "tp"), P("seq", "tp"))
    out_specs = (P("seq", "tp"), P("seq"))
    return jax.shard_map(shards, mesh=mesh, in_specs=in_specs, out_specs=out_specs, check_vma=False)
```

time: 361 us -> 159 us (0.44)
  waiting for transfers between devices: 294 us -> 0 us
  Pallas kernels: 0 us -> 155 us
  matrix products: 30.6 us -> 0 us
  blocking collectives: 13.8 us -> 0 us
  between operations: 14 us -> 0.65 us
  other arithmetic: 6.69 us -> 0 us
    all_gather x2 -> x0, waiting for transfers between devices: 293 us -> none  [the longest x1 150 us: shards(): gate = add_single(lax.all_gather(gate_weight, 'seq', axis=0, tiled=True))]
    pallas_call x0 -> x1, Pallas kernels: none -> 155 us  [shards(): pl.pallas_call(kernel, name='block', out_shape=(jax.ShapeDtypeStruct((TOK...]
    dot_general x2 -> x0, matrix products: 30.6 us -> none  [add_rows(): return jnp.dot(normed, piece, preferred_element_type=jnp.float32)]
    pmax x1 -> x0, blocking collectives: 13.8 us -> none  [shards(): scales = lax.pmax(local_peak, 'tp') + 1e-06]
    convert_element_type x1 -> x0, other arithmetic: 3.63 us -> none  [shards(): saved = (hidden / scales[:, None]).astype(jnp.bfloat16)]
  transfers between devices with their start and end apart: 2 -> 0, of which waited for: 2 -> 0; matrix products, arithmetic and copies ran while one was open for 5% -> 0% of each run, Pallas kernels for 0% -> 0%
where the time goes in v1:
time: 159 us
  Pallas kernels  155 us (97%)
  local copies, waits for them, and re-layouts  3.41 us (2%)
    pallas_call x1, Pallas kernels, shards(): pl.pallas_call(kernel, name='block', out_shape=(jax.ShapeDtypeStruct((TOK...  155 us
    unnamed x4, local copies, waits for them, and re-layouts  3.41 us

profile of v1, /device:TPU:1, one launch (start us, length us, event | category | flops | bytes accessed | tf_op | source)
XLA Modules:
  0.0 158.8 jit_solution(6908072423157172893)
XLA Ops:
  0.6 154.8 %block.1 = (bf16[504,1792]{1,0:T(8,128)(2,1)}, f32[504]{0:T(512)}) custom-call(bf16[504,4096]{1,0:T(8,128)(2,1)} %tok_hbm.1, f32[4096]{0:T(1024)} %gain_ref.1, bf16[64,1792]{1,0:T(8,128)(2,1)} %gate_hbm.1, bf16[64,1792]{1,0:T(8,128)(2,1)} %up_hbm.1), custom_call_target="tpu_custom_call" | custom-call | tf_op jit(solution)/shard_map/block/pallas_call | solution.py:407
  155.4 0.0 copy-start
  155.4 2.8 %copy.8 = bf16[504,1792]{1,0:T(8,128)(2,1)} copy(bf16[504,1792]{1,0:T(8,128)(2,1)} %get-tuple-element.4) | data formatting | bytes 3612672
  158.3 0.0 copy-done
  158.3 0.6 copy.9
Async XLA Ops:
  155.4 2.8 %copy-start = (f32[504]{0:T(512)S(1)}, f32[504]{0:T(512)}, u32[]{:S(2)}) copy-start(f32[504]{0:T(512)} %get-tuple-element.5) | copy-start | bytes 6052

commit v2 on v0

v2 whole, which is shorter than its diff:
```python
import jax
import jax.numpy as jnp
from jax import lax
from jax.experimental import pallas as pl
from jax.experimental.pallas import tpu as pltpu
from jax.sharding import PartitionSpec as P

MESH = pl.DeviceIdType.MESH
TOK = 504
PAD = 512
D = 4096
PIECE = 896
NCOL = 2 * PIECE
ROWS = 128
EPS = 1e-05
WIDTH = (256, 256, 256, 128)
START = (0, 256, 512, 768)
G = len(WIDTH)
ND, NQ = 1, 2


def mod(v, n):
    return lax.rem(v + 2 * n, n)


def kernel(tok_hbm, gain_ref, gate_hbm, up_hbm, out_ref, scale_ref,
           raw, tok, *rest):
    w = rest[:G]
    (peak, osend, orecv, psend, precv, raw_sem, s1_ss, s1_rs, t_ss, t_rs, f_ss, r_ss, r_rs, q_ss,
     z_ss, z_rs, y_ss, y_rs, b_ss, b_rs, o_ss, o_rs, p_ss, p_rs) = rest[G:]
    s = lax.axis_index("seq")
    t = lax.axis_index("tp")
    x = s % 4
    zh = (s // 4) % 4
    y = s // 16
    zl = t // 2
    c = t % 2

    def dev(xx, yy, zz, ll, cc):
        return ((yy * 4 + zz) * 4 + xx, ll * 2 + cc)

    def rc(src, dst, ssem, rsem, target):
        return pltpu.make_async_remote_copy(
            src_ref=src, dst_ref=dst, send_sem=ssem, recv_sem=rsem,
            device_id=target, device_id_type=MESH)

    xp, xm = mod(x + 1, 4), mod(x - 1, 4)
    yp, ym = mod(y + 1, 4), mod(y - 1, 4)
    zp, zm = mod(zh + 1, 4), mod(zh - 1, 4)
    sib = dev(x, y, zh, zl, 1 - c)
    pair = dev(x, y, zh, 1 - zl, c)
    y_up, y_dn = dev(x, yp, zh, zl, c), dev(x, ym, zh, zl, c)
    z_up, z_dn = dev(x, y, zp, zl, c), dev(x, y, zm, zl, c)

    raw_copy = pltpu.make_async_copy(tok_hbm, raw, raw_sem)
    raw_copy.start()

    barrier = pltpu.get_barrier_semaphore()
    for dx in range(4):
        for ll in range(2):
            for cc in range(2):
                if dx == 0 and ll == 0 and cc == 0:
                    continue
                pl.semaphore_signal(
                    barrier, inc=1, device_id_type=MESH,
                    device_id=dev(mod(x + dx, 4), y, zh, (zl + ll) % 2, (c + cc) % 2))
    for target in (y_up, y_dn, z_up, z_dn):
        pl.semaphore_signal(barrier, inc=1, device_id=target, device_id_type=MESH)

    raw_copy.wait()
    gain = gain_ref[...].reshape(1, D)

    def normed(values):
        v = values.astype(jnp.float32)
        mean_square = jnp.sum(v * v, axis=1, keepdims=True) * (1.0 / D)
        return (v * lax.rsqrt(mean_square + EPS) * gain).astype(jnp.bfloat16)

    def put(r, n, val):
        for yy in range(4):
            for zz in range(4):
                a, b = (yy * 4 + zz) * 256, (zz * 4 + yy) * 256
                tok[2, pl.ds(r, n), pl.ds(b, 256)] = val[:, a:a + 256]

    def norm_group(i, carry):
        r = pl.multiple_of(i * 16, 16)
        put(r, 16, normed(raw[pl.ds(r, 16), :]))
        return carry

    lax.fori_loop(0, 31, norm_group, 0)
    tail = normed(raw[pl.ds(496, 8), :])
    put(496, 16, jnp.concatenate([tail, jnp.zeros((8, D), jnp.bfloat16)], axis=0))
    peak[...] = jnp.zeros_like(peak)

    pl.semaphore_wait(barrier, 19)

    def chunk(g, zz, yy, cc):
        return w[g].at[zz * 4 + yy, cc]

    def half(g, zz, yy, hh):
        return w[g].at[zz * 4 + yy, c, pl.ds(hh * 64, 64)]

    def s1_dst(g, xx, u):
        return w[g].at[zh * 4 + y, xx // 2, pl.ds(pl.multiple_of((xx % 2) * 64, 64), 64),
                       pl.ds(u * WIDTH[g], WIDTH[g])]

    def s1_copy(g, h, u):
        src = (gate_hbm, up_hbm)[u].at[:, pl.ds(h * PIECE + START[g], WIDTH[g])]
        return src, s1_dst(g, x, u), s1_rs.at[g * 4 + (x % 2) * 2 + u]

    def s1_each(act):
        for g in range(G):
            for h in range(2):
                mine = jnp.logical_and(x // 2 == c, x % 2 == h)
                for u in range(2):
                    act(g, h, u, mine)

    def s1_start(g, h, u, mine):
        src, dst, sem = s1_copy(g, h, u)

        @pl.when(mine)
        def _():
            pltpu.make_async_copy(src, dst, sem).start()

        @pl.when(jnp.logical_not(mine))
        def _():
            rc(src, dst, s1_ss.at[g * 4 + h * 2 + u], sem, dev(2 * c + h, y, zh, zl, x // 2)).start()

    def s1_sent(g, h, u, mine):
        src, dst, sem = s1_copy(g, h, u)

        @pl.when(jnp.logical_not(mine))
        def _():
            rc(src, dst, s1_ss.at[g * 4 + h * 2 + u], sem, sib).wait_send()

    s1_each(s1_start)

    def tok_half(slot, q):
        return tok.at[slot, pl.ds(pl.multiple_of(jnp.where(zl == 0, q, 7 - q) * 64, 64), 64)]

    t_target = dev(mod(x + 1 - 2 * c, 4), y, zh, zl, 1)

    def t_send(q):
        return rc(tok_half(2, q), tok_half(c, q), t_ss.at[q], t_rs.at[c * 8 + q], t_target)

    for q in range(8 - ND):
        t_send(q).start()

    def t_arrived(slot, q):
        ref = tok_half(slot, q)
        rc(ref, ref, t_ss.at[0], t_rs.at[slot * 8 + q], sib).wait_recv()

    def t_copy(slot, q):
        ref = tok_half(slot, q)
        return rc(ref, ref, f_ss.at[slot * 2 + q], t_rs.at[slot * 8 + 7 - q], pair)

    def relay(q):
        slot = q % 2
        target = dev((xp, xm)[slot], y, zh, zl, 0)
        return rc(tok_half(slot, q), tok_half(1, q), r_ss.at[q], r_rs.at[q], target)

    def opp_arrived(q):
        ref = tok_half(1, q)
        rc(ref, ref, r_ss.at[0], r_rs.at[q], sib).wait_recv()

    def opp_copy(q):
        ref = tok_half(1, q)
        return rc(ref, ref, q_ss.at[q], r_rs.at[7 - q], pair)

    def t_step(q):
        @pl.when(c == 1)
        def _():
            for slot in range(2):
                t_arrived(slot, q)
            if q < 8 - NQ:
                relay(q).start()

    def t_pass(slot, q):
        @pl.when(c == 1)
        def _():
            t_copy(slot, q).start()

    def t_last():
        @pl.when(c == 1)
        def _():
            for slot in range(2):
                for q in range(8 - ND, 8):
                    t_arrived(slot, q)

    def q_pass(q):
        @pl.when(c == 0)
        def _():
            opp_arrived(q)
            opp_copy(q).start()

    def q_last():
        @pl.when(c == 0)
        def _():
            for q in range(NQ, 8):
                opp_arrived(q)

    rels = (0, 1, 3, 2)
    zz_of = {r: mod(zh + r, 4) for r in rels}
    yy_of = {0: y, 1: yp, 3: ym, 2: mod(y + 2, 4)}

    def b_copy(g, r, cc):
        ref = w[g].at[pl.ds(pl.multiple_of(zz_of[r] * 4, 4), 4), cc]
        return rc(ref, ref, b_ss.at[g * 4 + r], b_rs.at[g * 4 + r], sib)

    def b_wait(g):
        for r in rels:
            b_copy(g, r, 1 - c).wait_recv()

    def y_copy(g, r, d):
        ref = chunk(g, zz_of[r], y, c)
        i = (g * 4 + r) * 4 + d
        return rc(ref, ref, y_ss.at[i], y_rs.at[i], (y_up, y_dn)[d])

    def y_relay(g, r, d):
        ref = half(g, zz_of[r], (ym, yp)[d], d)
        i = (g * 4 + r) * 4 + 2 + d
        return rc(ref, ref, y_ss.at[i], y_rs.at[i], (y_up, y_dn)[d])

    def z_copy(g, d):
        ref = chunk(g, zh, y, c)
        return rc(ref, ref, z_ss.at[g * 4 + d], z_rs.at[g * 4 + d], (z_up, z_dn)[d])

    def z_relay(g, d):
        ref = half(g, (zm, zp)[d], y, d)
        return rc(ref, ref, z_ss.at[g * 4 + 2 + d], z_rs.at[g * 4 + 2 + d], (z_up, z_dn)[d])

    def own(g):
        for p in range(2):
            for u in range(2):
                ref = s1_dst(g, 2 * c + p, u)
                rc(ref, ref, s1_ss.at[0], s1_rs.at[g * 4 + p * 2 + u], sib).wait_recv()

    def z_send(g):
        for d in range(2):
            z_copy(g, d).start()

    def z_near(g):
        for d in range(2):
            ref = chunk(g, (zm, zp)[d], y, c)
            rc(ref, ref, z_ss.at[0], z_rs.at[g * 4 + d], sib).wait_recv()
            z_relay(g, d).start()

    def z_far(g):
        for d in range(2):
            ref = half(g, zz_of[2], y, d)
            rc(ref, ref, z_ss.at[0], z_rs.at[g * 4 + 2 + d], sib).wait_recv()

    def y_send(g, r):
        for d in range(2):
            y_copy(g, r, d).start()

    def y_near(g, r):
        for d in range(2):
            ref = chunk(g, zz_of[r], (ym, yp)[d], c)
            rc(ref, ref, y_ss.at[0], y_rs.at[(g * 4 + r) * 4 + d], sib).wait_recv()
            y_relay(g, r, d).start()

    def y_far(g, r):
        for d in range(2):
            ref = half(g, zz_of[r], yy_of[2], d)
            rc(ref, ref, y_ss.at[0], y_rs.at[(g * 4 + r) * 4 + 2 + d], sib).wait_recv()
        b_copy(g, r, c).start()

    first = jnp.where(c == 0, 2, 0)
    rel_of = (jnp.where(c == 0, 0, 3), jnp.where(c == 0, 2, 1))

    def move(rel, src, dst, ssem, rsem, ll, cc, wait):
        here = jnp.logical_and(rel == 0, jnp.logical_and(ll == zl, cc == c))

        @pl.when(jnp.logical_not(here))
        def _():
            copy = rc(src, dst, ssem, rsem, dev(mod(x + rel, 4), y, zh, ll, cc))
            if wait:
                copy.wait_send()
            else:
                copy.start()

        if not wait:
            @pl.when(here)
            def _():
                pltpu.make_async_copy(src, dst, rsem).start()

    def out_move(slot, g, wait=False):
        n = WIDTH[g]
        dst = orecv.at[:, pl.ds(pl.multiple_of((x % 2) * PIECE + START[g], 128), n)]
        move(rel_of[slot], osend.at[slot, :, pl.ds(START[g], n)], dst,
             o_ss.at[slot * G + g], o_rs.at[(x % 2) * G + g], zl, x // 2, wait)

    def peak_move(slot, wait=False):
        index = rel_of[slot] * 2 + zl
        for k in range(4):
            move(rel_of[slot], psend.at[slot], precv.at[index],
                 p_ss.at[slot * 4 + k], p_rs.at[index], k // 2, k % 2, wait)

    def unit(slot, g):
        n = WIDTH[g]
        src = first if slot == 0 else 1
        res = jnp.dot(tok[src], w[g][...].reshape(D, 2 * n), preferred_element_type=jnp.float32)
        gate, up = res[:, :n], res[:, n:]
        val = gate / (1.0 + jnp.exp(-gate)) * up
        top = peak[slot]
        for k in range(0, n, 128):
            top = jnp.maximum(top, jnp.abs(val[:, k:k + 128]))
        peak[slot] = top
        osend[slot, :, pl.ds(START[g], n)] = val.astype(jnp.bfloat16)
        if g < G - 1:
            out_move(slot, g)

    def on(core, *calls):
        @pl.when(c == core)
        def _():
            for slot, g in calls:
                unit(slot, g)

    def peak_out(slot):
        for i in range(4):
            r = pl.ds(i * 128, 128)
            top = jnp.max(peak[slot, r].T, axis=0, keepdims=True)
            psend[slot, :, r] = jnp.broadcast_to(top, (8, 128))
        peak_move(slot)

    own(0)
    y_send(0, 0)
    z_send(0)
    own(1)
    y_send(1, 0)
    own(2)
    y_send(2, 0)
    own(3)
    y_send(3, 0)
    y_near(0, 0)
    y_near(1, 0)
    z_near(0)
    z_send(1)
    y_send(0, 1)
    y_send(0, 3)
    t_step(0)
    t_pass(0, 0)
    t_pass(1, 0)
    y_near(2, 0)
    y_near(3, 0)
    y_far(0, 0)
    z_near(1)
    y_send(1, 1)
    t_step(1)
    y_send(1, 3)
    z_far(0)
    y_send(0, 2)
    y_far(1, 0)
    y_near(0, 1)
    y_near(0, 3)
    t_step(2)
    y_far(2, 0)
    t_step(3)
    y_far(3, 0)
    y_near(1, 1)
    y_near(1, 3)
    z_far(1)
    z_send(2)
    y_send(1, 2)
    t_step(4)
    y_near(0, 2)
    y_far(0, 1)
    y_far(0, 3)
    z_send(3)
    y_far(1, 1)
    z_near(2)
    y_send(2, 1)
    t_step(5)
    y_far(1, 3)
    y_send(2, 3)
    y_near(1, 2)
    y_far(0, 2)
    z_near(3)
    y_send(3, 1)
    y_send(3, 3)
    z_far(2)
    b_wait(0)
    y_send(2, 2)
    on(0, (0, 0))
    z_far(3)
    y_send(3, 2)
    t_step(6)
    t_last()
    on(1, (0, 0))
    y_near(2, 1)
    on(1, (1, 0))
    q_pass(0)
    q_pass(1)
    y_near(2, 3)
    y_far(1, 2)
    y_near(3, 1)
    y_near(3, 3)
    b_wait(1)
    on(0, (0, 1))
    on(1, (0, 1))
    y_near(2, 2)
    y_near(3, 2)
    on(1, (1, 1))
    y_far(2, 1)
    y_far(2, 3)
    y_far(3, 1)
    y_far(3, 3)
    y_far(2, 2)
    y_far(3, 2)
    q_last()
    on(0, (1, 0), (1, 1))
    b_wait(2)
    on(1, (0, 2), (1, 2))
    b_wait(3)
    on(0, (0, 2), (1, 2))
    unit(0, 3)
    unit(1, 3)
    peak_out(0)
    peak_out(1)
    out_move(0, G - 1)
    out_move(1, G - 1)

    s1_each(s1_sent)
    for q in range(8 - ND):
        t_send(q).wait_send()

    @pl.when(c == 1)
    def _():
        for q in range(8 - NQ):
            relay(q).wait_send()
        for slot in range(2):
            for q in range(ND):
                t_copy(slot, q).wait_send()

    @pl.when(c == 0)
    def _():
        for q in range(NQ):
            opp_copy(q).wait_send()

    for g in range(G):
        for d in range(2):
            z_copy(g, d).wait_send()
            z_relay(g, d).wait_send()
            for r in rels:
                y_copy(g, r, d).wait_send()
                y_relay(g, r, d).wait_send()
        for r in rels:
            b_copy(g, r, c).wait_send()

    for i in range(8):
        ref = precv.at[i]
        rc(ref, ref, p_ss.at[0], p_rs.at[i], sib).wait_recv()
    top = precv[0]
    for i in range(1, 8):
        top = jnp.maximum(top, precv[i])
    top = top + 1e-06
    scale_ref[...] = top[0, :TOK]
    inverse = 1.0 / top
    for p in range(2):
        for g in range(G):
            ref = orecv.at[:, pl.ds(p * PIECE + START[g], WIDTH[g])]
            rc(ref, ref, o_ss.at[0], o_rs.at[p * G + g], sib).wait_recv()
    for i in range(PAD // ROWS):
        n = min(ROWS, TOK - i * ROWS)
        inv = jnp.broadcast_to(inverse[:1, i * ROWS:(i + 1) * ROWS], (ROWS, ROWS)).T
        for k in range(NCOL // 128):
            val = orecv[pl.ds(i * ROWS, ROWS), pl.ds(k * 128, 128)].astype(jnp.float32) * inv
            out_ref[pl.ds(i * ROWS, n), pl.ds(k * 128, 128)] = val.astype(jnp.bfloat16)[:n]

    for slot in range(2):
        for g in range(G):
            out_move(slot, g, True)
        peak_move(slot, True)


def shards(tokens, norm_gain, gate_weight, up_weight):
    dma = pltpu.SemaphoreType.DMA
    vmem = pl.BlockSpec(memory_space=pltpu.VMEM)
    hbm = pl.BlockSpec(memory_space=pl.ANY)
    return pl.pallas_call(
        kernel,
        name="block",
        out_shape=(jax.ShapeDtypeStruct((TOK, NCOL), jnp.bfloat16),
                   jax.ShapeDtypeStruct((TOK,), jnp.float32)),
        in_specs=[hbm, vmem, hbm, hbm],
        out_specs=(vmem, vmem),
        scratch_shapes=[
            pltpu.VMEM((TOK, D), jnp.bfloat16),
            pltpu.VMEM((3, PAD, D), jnp.bfloat16),
            *[pltpu.VMEM((16, 2, 128, 2 * n), jnp.bfloat16) for n in WIDTH],
            pltpu.VMEM((2, PAD, 128), jnp.float32),
            pltpu.VMEM((2, PAD, PIECE), jnp.bfloat16),
            pltpu.VMEM((PAD, NCOL), jnp.bfloat16),
            pltpu.VMEM((2, 8, PAD), jnp.float32),
            pltpu.VMEM((8, 8, PAD), jnp.float32),
            dma, dma((G * 4,)), dma((G * 4,)), dma((8,)), dma((16,)), dma((4,)), dma((8,)), dma((8,)),
            dma((2,)), dma((G * 4,)), dma((G * 4,)), dma((G * 16,)), dma((G * 16,)),
            dma((G * 4,)), dma((G * 4,)), dma((2 * G,)), dma((2 * G,)), dma((8,)), dma((8,)),
        ],
        compiler_params=pltpu.CompilerParams(
            collective_id=0, has_side_effects=True, vmem_limit_bytes=58 * 2**20),
    )(tokens, norm_gain, gate_weight, up_weight)


def solution(mesh):
    in_specs = (P("seq", None), P(), P("seq", "tp"), P("seq", "tp"))
    out_specs = (P("seq", "tp"), P("seq"))
    return jax.shard_map(shards, mesh=mesh, in_specs=in_specs, out_specs=out_specs, check_vma=False)
```

time: 361 us -> 117 us (0.32)
  waiting for transfers between devices: 294 us -> 0 us
  Pallas kernels: 0 us -> 112 us
  matrix products: 30.6 us -> 0 us
  blocking collectives: 13.8 us -> 0 us
  between operations: 14 us -> 0.65 us
  other arithmetic: 6.69 us -> 0 us
    all_gather x2 -> x0, waiting for transfers between devices: 293 us -> none  [the longest x1 150 us: shards(): gate = add_single(lax.all_gather(gate_weight, 'seq', axis=0, tiled=True))]
    pallas_call x0 -> x1, Pallas kernels: none -> 112 us  [shards(): pl.pallas_call(kernel, name='block', out_shape=(jax.ShapeDtypeStruct((TOK...]
    dot_general x2 -> x0, matrix products: 30.6 us -> none  [add_rows(): return jnp.dot(normed, piece, preferred_element_type=jnp.float32)]
    pmax x1 -> x0, blocking collectives: 13.8 us -> none  [shards(): scales = lax.pmax(local_peak, 'tp') + 1e-06]
    convert_element_type x1 -> x0, other arithmetic: 3.63 us -> none  [shards(): saved = (hidden / scales[:, None]).astype(jnp.bfloat16)]
  transfers between devices with their start and end apart: 2 -> 0, of which waited for: 2 -> 0; matrix products, arithmetic and copies ran while one was open for 5% -> 0% of each run, Pallas kernels for 0% -> 0%
where the time goes in v2:
time: 117 us
  Pallas kernels  112 us (96%)
  local copies, waits for them, and re-layouts  3.41 us (3%)
    pallas_call x1, Pallas kernels, shards(): pl.pallas_call(kernel, name='block', out_shape=(jax.ShapeDtypeStruct((TOK...  112 us
    unnamed x4, local copies, waits for them, and re-layouts  3.41 us

profile of v2, /device:TPU:1, one launch (start us, length us, event | category | flops | bytes accessed | tf_op | source)
XLA Modules:
  0.0 116.5 jit_solution(18051658504900421314)
XLA Ops:
  0.6 112.4 %block.1 = (bf16[504,1792]{1,0:T(8,128)(2,1)}, f32[504]{0:T(512)}) custom-call(bf16[504,4096]{1,0:T(8,128)(2,1)} %tok_hbm.1, f32[4096]{0:T(1024)} %gain_ref.1, bf16[64,1792]{1,0:T(8,128)(2,1)} %gate_hbm.1, bf16[64,1792]{1,0:T(8,128)(2,1)} %up_hbm.1), custom_call_target="tpu_custom_call" | custom-call | tf_op jit(solution)/shard_map/block/pallas_call | solution.py:480
  113.1 0.0 copy-start
  113.1 2.8 %copy.8 = bf16[504,1792]{1,0:T(8,128)(2,1)} copy(bf16[504,1792]{1,0:T(8,128)(2,1)} %get-tuple-element.4) | data formatting | bytes 3612672
  115.9 0.0 copy-done
  115.9 0.6 copy.9
Async XLA Ops:
  113.1 2.8 %copy-start = (f32[504]{0:T(512)S(1)}, f32[504]{0:T(512)}, u32[]{:S(2)}) copy-start(f32[504]{0:T(512)} %get-tuple-element.5) | copy-start | bytes 6052

commit v3 on v2

--- a/solution.py
+++ b/solution.py
@@ -23,10 +23,10 @@
     return lax.rem(v + 2 * n, n)
 
 
-def kernel(tok_hbm, gain_ref, gate_hbm, up_hbm, out_ref, scale_ref,
+def kernel(tok_hbm, gain_ref, gate_hbm, up_hbm, orecv, top_ref,
            raw, tok, *rest):
     w = rest[:G]
-    (peak, osend, orecv, psend, precv, raw_sem, s1_ss, s1_rs, t_ss, t_rs, f_ss, r_ss, r_rs, q_ss,
+    (peak, osend, psend, precv, raw_sem, s1_ss, s1_rs, t_ss, t_rs, f_ss, r_ss, r_rs, q_ss,
      z_ss, z_rs, y_ss, y_rs, b_ss, b_rs, o_ss, o_rs, p_ss, p_rs) = rest[G:]
     s = lax.axis_index("seq")
     t = lax.axis_index("tp")
@@ -142,7 +142,7 @@
     def t_send(q):
         return rc(tok_half(2, q), tok_half(c, q), t_ss.at[q], t_rs.at[c * 8 + q], t_target)
 
-    for q in range(8 - ND):
+    def x_send(q):
         t_send(q).start()
 
     def t_arrived(slot, q):
@@ -192,10 +192,16 @@
             opp_arrived(q)
             opp_copy(q).start()
 
+    def q_mid():
+        @pl.when(c == 0)
+        def _():
+            for q in range(NQ, 4):
+                opp_arrived(q)
+
     def q_last():
         @pl.when(c == 0)
         def _():
-            for q in range(NQ, 8):
+            for q in range(4, 8):
                 opp_arrived(q)
 
     rels = (0, 1, 3, 2)
@@ -296,25 +302,27 @@
             move(rel_of[slot], psend.at[slot], precv.at[index],
                  p_ss.at[slot * 4 + k], p_rs.at[index], k // 2, k % 2, wait)
 
-    def unit(slot, g):
+    def unit(slot, g, part=None):
         n = WIDTH[g]
         src = first if slot == 0 else 1
-        res = jnp.dot(tok[src], w[g][...].reshape(D, 2 * n), preferred_element_type=jnp.float32)
+        rows = pl.ds(0, PAD) if part is None else pl.ds(
+            pl.multiple_of(jnp.where(zl == 0, part, 1 - part) * 256, 256), 256)
+        res = jnp.dot(tok[src, rows], w[g][...].reshape(D, 2 * n), preferred_element_type=jnp.float32)
         gate, up = res[:, :n], res[:, n:]
         val = gate / (1.0 + jnp.exp(-gate)) * up
-        top = peak[slot]
+        top = peak[slot, rows]
         for k in range(0, n, 128):
             top = jnp.maximum(top, jnp.abs(val[:, k:k + 128]))
-        peak[slot] = top
-        osend[slot, :, pl.ds(START[g], n)] = val.astype(jnp.bfloat16)
-        if g < G - 1:
+        peak[slot, rows] = top
+        osend[slot, rows, pl.ds(START[g], n)] = val.astype(jnp.bfloat16)
+        if g < G - 1 and part != 0:
             out_move(slot, g)
 
     def on(core, *calls):
         @pl.when(c == core)
         def _():
-            for slot, g in calls:
-                unit(slot, g)
+            for call in calls:
+                unit(*call)
 
     def peak_out(slot):
         for i in range(4):
@@ -323,9 +331,11 @@
             psend[slot, :, r] = jnp.broadcast_to(top, (8, 128))
         peak_move(slot)
 
+    x_send(0)
     own(0)
     y_send(0, 0)
     z_send(0)
+    x_send(1)
     own(1)
     y_send(1, 0)
     own(2)
@@ -333,88 +343,97 @@
     own(3)
     y_send(3, 0)
     y_near(0, 0)
+    x_send(2)
     y_near(1, 0)
+    z_send(1)
     z_near(0)
-    z_send(1)
-    y_send(0, 1)
     y_send(0, 3)
     t_step(0)
-    t_pass(0, 0)
-    t_pass(1, 0)
+    y_send(0, 1)
     y_near(2, 0)
     y_near(3, 0)
     y_far(0, 0)
+    t_step(1)
     z_near(1)
-    y_send(1, 1)
-    t_step(1)
     y_send(1, 3)
     z_far(0)
+    y_far(1, 0)
+    x_send(3)
+    z_send(2)
+    y_near(0, 3)
     y_send(0, 2)
-    y_far(1, 0)
+    t_step(2)
     y_near(0, 1)
-    y_near(0, 3)
-    t_step(2)
     y_far(2, 0)
+    z_far(1)
+    y_send(1, 1)
+    y_far(3, 0)
+    z_send(3)
+    z_near(2)
+    y_send(1, 2)
+    y_near(1, 3)
+    t_pass(0, 0)
+    x_send(4)
+    z_near(3)
+    y_far(0, 3)
+    z_far(2)
+    y_near(0, 2)
     t_step(3)
-    y_far(3, 0)
+    y_far(0, 1)
     y_near(1, 1)
-    y_near(1, 3)
-    z_far(1)
-    z_send(2)
-    y_send(1, 2)
+    x_send(5)
+    q_pass(0)
+    y_send(2, 3)
+    z_far(3)
+    y_near(1, 2)
+    y_far(1, 3)
+    y_send(2, 1)
+    x_send(6)
+    t_pass(1, 0)
+    y_send(2, 2)
     t_step(4)
-    y_near(0, 2)
-    y_far(0, 1)
-    y_far(0, 3)
-    z_send(3)
+    y_far(0, 2)
+    y_send(3, 3)
+    b_wait(0)
     y_far(1, 1)
-    z_near(2)
-    y_send(2, 1)
+    on(0, (0, 0))
+    y_send(3, 1)
+    y_near(2, 3)
+    y_send(3, 2)
     t_step(5)
-    y_far(1, 3)
-    y_send(2, 3)
-    y_near(1, 2)
-    y_far(0, 2)
-    z_near(3)
-    y_send(3, 1)
-    y_send(3, 3)
-    z_far(2)
-    b_wait(0)
-    y_send(2, 2)
-    on(0, (0, 0))
-    z_far(3)
-    y_send(3, 2)
+    q_pass(1)
+    y_far(1, 2)
+    y_near(2, 1)
+    b_wait(1)
+    on(0, (0, 1))
+    y_near(2, 2)
     t_step(6)
     t_last()
     on(1, (0, 0))
-    y_near(2, 1)
+    q_mid()
+    on(0, (1, 0, 0))
+    y_far(2, 3)
+    y_near(3, 3)
+    y_near(3, 1)
+    y_near(3, 2)
     on(1, (1, 0))
-    q_pass(0)
-    q_pass(1)
-    y_near(2, 3)
-    y_far(1, 2)
-    y_near(3, 1)
-    y_near(3, 3)
-    b_wait(1)
-    on(0, (0, 1))
+    on(0, (1, 1, 0))
+    q_last()
+    on(0, (1, 0, 1))
+    y_far(2, 1)
+    y_far(2, 2)
+    on(0, (1, 1, 1))
+    y_far(3, 3)
+    y_far(3, 1)
+    y_far(3, 2)
     on(1, (0, 1))
-    y_near(2, 2)
-    y_near(3, 2)
+    b_wait(2)
+    on(0, (0, 2))
     on(1, (1, 1))
-    y_far(2, 1)
-    y_far(2, 3)
-    y_far(3, 1)
-    y_far(3, 3)
-    y_far(2, 2)
-    y_far(3, 2)
-    q_last()
-    on(0, (1, 0), (1, 1))
-    b_wait(2)
-    on(1, (0, 2), (1, 2))
     b_wait(3)
-    on(0, (0, 2), (1, 2))
+    on(0, (1, 2, 0), (1, 2, 1), (1, 3, 0), (1, 3, 1))
+    on(1, (0, 2), (1, 2), (1, 3))
     unit(0, 3)
-    unit(1, 3)
     peak_out(0)
     peak_out(1)
     out_move(0, G - 1)
@@ -453,19 +472,11 @@
     top = precv[0]
     for i in range(1, 8):
         top = jnp.maximum(top, precv[i])
-    top = top + 1e-06
-    scale_ref[...] = top[0, :TOK]
-    inverse = 1.0 / top
+    top_ref[...] = top + 1e-06
     for p in range(2):
         for g in range(G):
             ref = orecv.at[:, pl.ds(p * PIECE + START[g], WIDTH[g])]
             rc(ref, ref, o_ss.at[0], o_rs.at[p * G + g], sib).wait_recv()
-    for i in range(PAD // ROWS):
-        n = min(ROWS, TOK - i * ROWS)
-        inv = jnp.broadcast_to(inverse[:1, i * ROWS:(i + 1) * ROWS], (ROWS, ROWS)).T
-        for k in range(NCOL // 128):
-            val = orecv[pl.ds(i * ROWS, ROWS), pl.ds(k * 128, 128)].astype(jnp.float32) * inv
-            out_ref[pl.ds(i * ROWS, n), pl.ds(k * 128, 128)] = val.astype(jnp.bfloat16)[:n]
 
     for slot in range(2):
         for g in range(G):
@@ -473,33 +484,55 @@
         peak_move(slot, True)
 
 
+def rescale(hidden_ref, top_ref, all_ref, out_ref, scale_ref):
+    inv = jnp.broadcast_to(1.0 / top_ref[:1, :], (ROWS, ROWS)).T
+    for k in range(0, NCOL, 128):
+        cols = pl.ds(k, 128)
+        out_ref[:, cols] = (hidden_ref[:, cols].astype(jnp.float32) * inv).astype(jnp.bfloat16)
+
+    @pl.when(pl.program_id(0) == 0)
+    def _():
+        scale_ref[...] = all_ref[0, :TOK]
+
+
 def shards(tokens, norm_gain, gate_weight, up_weight):
     dma = pltpu.SemaphoreType.DMA
     vmem = pl.BlockSpec(memory_space=pltpu.VMEM)
     hbm = pl.BlockSpec(memory_space=pl.ANY)
-    return pl.pallas_call(
+    hidden, tops = pl.pallas_call(
         kernel,
         name="block",
-        out_shape=(jax.ShapeDtypeStruct((TOK, NCOL), jnp.bfloat16),
-                   jax.ShapeDtypeStruct((TOK,), jnp.float32)),
+        out_shape=(jax.ShapeDtypeStruct((PAD, NCOL), jnp.bfloat16),
+                   jax.ShapeDtypeStruct((8, PAD), jnp.float32)),
         in_specs=[hbm, vmem, hbm, hbm],
-        out_specs=(vmem, vmem),
+        out_specs=(hbm, vmem),
         scratch_shapes=[
             pltpu.VMEM((TOK, D), jnp.bfloat16),
             pltpu.VMEM((3, PAD, D), jnp.bfloat16),
             *[pltpu.VMEM((16, 2, 128, 2 * n), jnp.bfloat16) for n in WIDTH],
             pltpu.VMEM((2, PAD, 128), jnp.float32),
             pltpu.VMEM((2, PAD, PIECE), jnp.bfloat16),
-            pltpu.VMEM((PAD, NCOL), jnp.bfloat16),
             pltpu.VMEM((2, 8, PAD), jnp.float32),
             pltpu.VMEM((8, 8, PAD), jnp.float32),
             dma, dma((G * 4,)), dma((G * 4,)), dma((8,)), dma((16,)), dma((4,)), dma((8,)), dma((8,)),
-            dma((2,)), dma((G * 4,)), dma((G * 4,)), dma((G * 16,)), dma((G * 16,)),
+            dma((4,)), dma((G * 4,)), dma((G * 4,)), dma((G * 16,)), dma((G * 16,)),
             dma((G * 4,)), dma((G * 4,)), dma((2 * G,)), dma((2 * G,)), dma((8,)), dma((8,)),
         ],
         compiler_params=pltpu.CompilerParams(
             collective_id=0, has_side_effects=True, vmem_limit_bytes=58 * 2**20),
     )(tokens, norm_gain, gate_weight, up_weight)
+    return pl.pallas_call(
+        rescale,
+        name="rescale",
+        grid=(PAD // ROWS,),
+        out_shape=(jax.ShapeDtypeStruct((TOK, NCOL), jnp.bfloat16),
+                   jax.ShapeDtypeStruct((TOK,), jnp.float32)),
+        in_specs=[pl.BlockSpec((ROWS, NCOL), lambda i: (i, 0)),
+                  pl.BlockSpec((8, ROWS), lambda i: (0, i)),
+                  pl.BlockSpec((8, PAD), lambda i: (0, 0))],
+        out_specs=(pl.BlockSpec((ROWS, NCOL), lambda i: (i, 0)),
+                   pl.BlockSpec((TOK,), lambda i: (0,))),
+    )(hidden, tops, tops)
 
 
 def solution(mesh):

time: 117 us -> 111 us (0.949)
  local copies, waits for them, and re-layouts: 3.41 us -> 0 us
  Pallas kernels: 112 us -> 110 us
    unnamed x4 -> x0, local copies, waits for them, and re-layouts: 3.41 us -> none
    pallas_call x1 -> x2, Pallas kernels: 112 us -> 110 us  [the longest x1 106 us: shards(): pl.pallas_call(kernel, name='block', out_shape=(jax.ShapeDtypeStruct((PAD...]
where the time goes in v3:
time: 111 us
  Pallas kernels  110 us (99%)
    pallas_call x1, Pallas kernels, shards(): pl.pallas_call(kernel, name='block', out_shape=(jax.ShapeDtypeStruct((PAD...  106 us
    pallas_call x1, Pallas kernels, shards(): pl.pallas_call(rescale, name='rescale', grid=(PAD // ROWS,), out_shape=(j...  3.95 us

profile of v3, /device:TPU:1, one launch (start us, length us, event | category | flops | bytes accessed | tf_op | source)
XLA Modules:
  0.0 110.9 jit_solution(1741033618769844071)
XLA Ops:
  0.6 106.3 %block.1 = (bf16[512,1792]{1,0:T(8,128)(2,1)}, f32[8,512]{1,0:T(8,128)}) custom-call(bf16[504,4096]{1,0:T(8,128)(2,1)} %tok_hbm.1, f32[4096]{0:T(1024)} %gain_ref.1, bf16[64,1792]{1,0:T(8,128)(2,1)} %gate_hbm.1, bf16[64,1792]{1,0:T(8,128)(2,1)} %up_hbm.1), custom_call_target="tpu_custom_call" | custom-call | tf_op jit(solution)/shard_map/block/pallas_call | solution.py:502
  106.9 3.9 %rescale.1 = (bf16[504,1792]{1,0:T(8,128)(2,1)}, f32[504]{0:T(512)}) custom-call(bf16[512,1792]{1,0:T(8,128)(2,1)} %get-tuple-element.4.hidden_ref, f32[8,512]{1,0:T(8,128)} %get-tuple-element.5.top_ref.all_ref, f32[8,512]{1,0:T(8,128)} %get-tuple-element.5.top_ref.all_ref), custom_call_target="tpu_custom_call" | custom-call | tf_op jit(solution)/shard_map/rescale/pallas_call | solution.py:524

commit v4 on v3

--- a/solution.py
+++ b/solution.py
@@ -12,6 +12,7 @@
 PIECE = 896
 NCOL = 2 * PIECE
 ROWS = 128
+BLOCK = 256
 EPS = 1e-05
 WIDTH = (256, 256, 256, 128)
 START = (0, 256, 512, 768)
@@ -315,7 +316,7 @@
             top = jnp.maximum(top, jnp.abs(val[:, k:k + 128]))
         peak[slot, rows] = top
         osend[slot, rows, pl.ds(START[g], n)] = val.astype(jnp.bfloat16)
-        if g < G - 1 and part != 0:
+        if part != 0:
             out_move(slot, g)
 
     def on(core, *calls):
@@ -344,8 +345,8 @@
     y_send(3, 0)
     y_near(0, 0)
     x_send(2)
+    z_send(1)
     y_near(1, 0)
-    z_send(1)
     z_near(0)
     y_send(0, 3)
     t_step(0)
@@ -436,8 +437,6 @@
     unit(0, 3)
     peak_out(0)
     peak_out(1)
-    out_move(0, G - 1)
-    out_move(1, G - 1)
 
     s1_each(s1_sent)
     for q in range(8 - ND):
@@ -485,10 +484,12 @@
 
 
 def rescale(hidden_ref, top_ref, all_ref, out_ref, scale_ref):
-    inv = jnp.broadcast_to(1.0 / top_ref[:1, :], (ROWS, ROWS)).T
-    for k in range(0, NCOL, 128):
-        cols = pl.ds(k, 128)
-        out_ref[:, cols] = (hidden_ref[:, cols].astype(jnp.float32) * inv).astype(jnp.bfloat16)
+    for r in range(0, BLOCK, ROWS):
+        rows = pl.ds(r, ROWS)
+        inv = jnp.broadcast_to(1.0 / top_ref[:1, r:r + ROWS], (ROWS, ROWS)).T
+        for k in range(0, NCOL, 128):
+            cols = pl.ds(k, 128)
+            out_ref[rows, cols] = (hidden_ref[rows, cols].astype(jnp.float32) * inv).astype(jnp.bfloat16)
 
     @pl.when(pl.program_id(0) == 0)
     def _():
@@ -524,13 +525,13 @@
     return pl.pallas_call(
         rescale,
         name="rescale",
-        grid=(PAD // ROWS,),
+        grid=(PAD // BLOCK,),
         out_shape=(jax.ShapeDtypeStruct((TOK, NCOL), jnp.bfloat16),
                    jax.ShapeDtypeStruct((TOK,), jnp.float32)),
-        in_specs=[pl.BlockSpec((ROWS, NCOL), lambda i: (i, 0)),
-                  pl.BlockSpec((8, ROWS), lambda i: (0, i)),
+        in_specs=[pl.BlockSpec((BLOCK, NCOL), lambda i: (i, 0)),
+                  pl.BlockSpec((8, BLOCK), lambda i: (0, i)),
                   pl.BlockSpec((8, PAD), lambda i: (0, 0))],
-        out_specs=(pl.BlockSpec((ROWS, NCOL), lambda i: (i, 0)),
+        out_specs=(pl.BlockSpec((BLOCK, NCOL), lambda i: (i, 0)),
                    pl.BlockSpec((TOK,), lambda i: (0,))),
     )(hidden, tops, tops)
 

time: 111 us -> 108 us (0.973)
  Pallas kernels: 110 us -> 107 us
    pallas_call x1, Pallas kernels: 106 us -> 104 us  [shards(): pl.pallas_call(kernel, name='block', out_shape=(jax.ShapeDtypeStruct((PAD...]
    pallas_call x1, Pallas kernels: 3.95 us -> 2.76 us  [shards(): pl.pallas_call(rescale, name='rescale', grid=(PAD // BLOCK,), out_shape=(...]
where the time goes in v4:
time: 108 us
  Pallas kernels  107 us (99%)
    pallas_call x1, Pallas kernels, shards(): pl.pallas_call(kernel, name='block', out_shape=(jax.ShapeDtypeStruct((PAD...  104 us
    pallas_call x1, Pallas kernels, shards(): pl.pallas_call(rescale, name='rescale', grid=(PAD // BLOCK,), out_shape=(...  2.76 us

profile of v4, /device:TPU:1, one launch (start us, length us, event | category | flops | bytes accessed | tf_op | source)
XLA Modules:
  0.0 107.8 jit_solution(15019921201519128310)
XLA Ops:
  0.6 104.4 %block.1 = (bf16[512,1792]{1,0:T(8,128)(2,1)}, f32[8,512]{1,0:T(8,128)}) custom-call(bf16[504,4096]{1,0:T(8,128)(2,1)} %tok_hbm.1, f32[4096]{0:T(1024)} %gain_ref.1, bf16[64,1792]{1,0:T(8,128)(2,1)} %gate_hbm.1, bf16[64,1792]{1,0:T(8,128)(2,1)} %up_hbm.1), custom_call_target="tpu_custom_call" | custom-call | tf_op jit(solution)/shard_map/block/pallas_call | solution.py:503
  105.1 2.8 %rescale.1 = (bf16[504,1792]{1,0:T(8,128)(2,1)}, f32[504]{0:T(512)}) custom-call(bf16[512,1792]{1,0:T(8,128)(2,1)} %get-tuple-element.4.hidden_ref, f32[8,512]{1,0:T(8,128)} %get-tuple-element.5.top_ref.all_ref, f32[8,512]{1,0:T(8,128)} %get-tuple-element.5.top_ref.all_ref), custom_call_target="tpu_custom_call" | custom-call | tf_op jit(solution)/shard_map/rescale/pallas_call | solution.py:525

commit v5 on v4

--- a/solution.py
+++ b/solution.py
@@ -68,30 +68,6 @@
     for target in (y_up, y_dn, z_up, z_dn):
         pl.semaphore_signal(barrier, inc=1, device_id=target, device_id_type=MESH)
 
-    raw_copy.wait()
-    gain = gain_ref[...].reshape(1, D)
-
-    def normed(values):
-        v = values.astype(jnp.float32)
-        mean_square = jnp.sum(v * v, axis=1, keepdims=True) * (1.0 / D)
-        return (v * lax.rsqrt(mean_square + EPS) * gain).astype(jnp.bfloat16)
-
-    def put(r, n, val):
-        for yy in range(4):
-            for zz in range(4):
-                a, b = (yy * 4 + zz) * 256, (zz * 4 + yy) * 256
-                tok[2, pl.ds(r, n), pl.ds(b, 256)] = val[:, a:a + 256]
-
-    def norm_group(i, carry):
-        r = pl.multiple_of(i * 16, 16)
-        put(r, 16, normed(raw[pl.ds(r, 16), :]))
-        return carry
-
-    lax.fori_loop(0, 31, norm_group, 0)
-    tail = normed(raw[pl.ds(496, 8), :])
-    put(496, 16, jnp.concatenate([tail, jnp.zeros((8, D), jnp.bfloat16)], axis=0))
-    peak[...] = jnp.zeros_like(peak)
-
     pl.semaphore_wait(barrier, 19)
 
     def chunk(g, zz, yy, cc):
@@ -134,6 +110,31 @@
             rc(src, dst, s1_ss.at[g * 4 + h * 2 + u], sem, sib).wait_send()
 
     s1_each(s1_start)
+
+    raw_copy.wait()
+    gain = gain_ref[...].reshape(1, D)
+
+    def normed(values):
+        v = values.astype(jnp.float32)
+        mean_square = jnp.sum(v * v, axis=1, keepdims=True) * (1.0 / D)
+        return (v * lax.rsqrt(mean_square + EPS) * gain).astype(jnp.bfloat16)
+
+    def put(r, n, val):
+        for yy in range(4):
+            for zz in range(4):
+                a, b = (yy * 4 + zz) * 256, (zz * 4 + yy) * 256
+                tok[2, pl.ds(r, n), pl.ds(b, 256)] = val[:, a:a + 256]
+
+    def norm_group(i, carry):
+        r = pl.multiple_of(i * 16, 16)
+        put(r, 16, normed(raw[pl.ds(r, 16), :]))
+        return carry
+
+    lax.fori_loop(0, 31, norm_group, 0)
+    tail = normed(raw[pl.ds(496, 8), :])
+    put(496, 16, jnp.concatenate([tail, jnp.zeros((8, D), jnp.bfloat16)], axis=0))
+    peak[...] = jnp.zeros_like(peak)
+
 
     def tok_half(slot, q):
         return tok.at[slot, pl.ds(pl.multiple_of(jnp.where(zl == 0, q, 7 - q) * 64, 64), 64)]

time: 108 us -> 107 us (level)
  no operation moved by 1% of the time
where the time goes in v5:
time: 107 us
  Pallas kernels  106 us (99%)
    pallas_call x1, Pallas kernels, shards(): pl.pallas_call(kernel, name='block', out_shape=(jax.ShapeDtypeStruct((PAD...  104 us
    pallas_call x1, Pallas kernels, shards(): pl.pallas_call(rescale, name='rescale', grid=(PAD // BLOCK,), out_shape=(...  2.76 us

profile of v5, /device:TPU:1, one launch (start us, length us, event | category | flops | bytes accessed | tf_op | source)
XLA Modules:
  0.0 107.0 jit_solution(9611615785035249058)
XLA Ops:
  0.6 103.6 %block.1 = (bf16[512,1792]{1,0:T(8,128)(2,1)}, f32[8,512]{1,0:T(8,128)}) custom-call(bf16[504,4096]{1,0:T(8,128)(2,1)} %tok_hbm.1, f32[4096]{0:T(1024)} %gain_ref.1, bf16[64,1792]{1,0:T(8,128)(2,1)} %gate_hbm.1, bf16[64,1792]{1,0:T(8,128)(2,1)} %up_hbm.1), custom_call_target="tpu_custom_call" | custom-call | tf_op jit(solution)/shard_map/block/pallas_call | solution.py:504
  104.2 2.8 %rescale.1 = (bf16[504,1792]{1,0:T(8,128)(2,1)}, f32[504]{0:T(512)}) custom-call(bf16[512,1792]{1,0:T(8,128)(2,1)} %get-tuple-element.4.hidden_ref, f32[8,512]{1,0:T(8,128)} %get-tuple-element.5.top_ref.all_ref, f32[8,512]{1,0:T(8,128)} %get-tuple-element.5.top_ref.all_ref), custom_call_target="tpu_custom_call" | custom-call | tf_op jit(solution)/shard_map/rescale/pallas_call | solution.py:526
